TPU v7x, 512 devices: a whole 4x4x16 slice. The times are simulated.
512 devices in a mesh: ctx: 32 (over z, core), inner: 16 (over y, x).
Axes of the slice: x: 4, y: 4, z: 16, core: 2. Of those that a mesh axis runs over, the one named last changes fastest.
Arguments:
- tokens: bfloat16 [65536, 2048], P(('ctx', 'inner')), may hold values from -6 to 6
- project_weight: bfloat16 [2048, 2, 4096], P('ctx', None, 'inner'), may hold values from -0.125 to 0.125
- state_weight: bfloat16 [2048, 2, 512], P('ctx', None, 'inner'), may hold values from -0.125 to 0.125
- step_weight: bfloat16 [2048, 64], P('ctx', 'inner'), may hold values from -0.125 to 0.125
- mixer_taps: float32 [5, 4096], P(None, 'inner'), may hold values from -2.5 to 2.5
- state_taps: float32 [5, 2, 512], replicated, may hold values from -2.5 to 2.5
- step_bias: float32 [64], P('inner'), may hold values from -4.6 to -2.3
- decay_log: float32 [64], P('inner'), may hold values from -13 to 0.5, as said below
- norm_gain: float32 [4096], replicated, may hold values from 0.1 to 1.9
Outputs:
- mixed_output: bfloat16 [65536, 4096], P(('ctx', 'inner'))
Inputs may be any that keep to these rules, and one draw needn't show every extreme that they name: `decay_log`: one value a head.
All inputs are finite; a program needn't handle non-finite values.
Results may differ from a plain program's by a relative error of at most 0.0075.
Values may be sent and summed in bfloat16 or wider, within the bound.
A program may use at most 64 MiB of HBM per device.

v0:
```python
import jax
import jax.numpy as jnp
from jax import lax
from jax.sharding import PartitionSpec as P

H = 64
P_SIZE = 64
N = 128
G = 4
CONV = 4
SPAN = 128
EPSILON = 1e-05


def passed_along(x, axis, by):
    count = lax.axis_size(axis)
    pairs = [(i, i + by) for i in range(count) if 0 <= i + by < count]
    return lax.ppermute(x, axis, pairs)


def entering(x, axis, join, neutral):
    place = lax.axis_index(axis)
    gathered = jax.tree.map(
        lambda a, kind: lax.all_gather(a.astype(kind), axis), x, (jnp.bfloat16, jnp.bfloat16)
    )
    state = jax.tree.map(lambda a, e: jnp.zeros_like(a) + jnp.asarray(e, a.dtype), x, neutral)

    def one(turn, state):
        return join(
            state,
            jax.tree.map(
                lambda a, own: lax.dynamic_index_in_dim(a, turn, 0, False).astype(own.dtype),
                gathered,
                x,
            ),
        )

    return lax.fori_loop(0, place, one, state)


def partner(value, axis, stride):
    mask = 2**stride
    pairs = [(source, source ^ mask) for source in range(lax.axis_size(axis))]
    return lax.ppermute(value, axis, pairs)


def conv_apply(taps, previous, current):
    extended = jnp.concatenate([previous, current], axis=0)
    length_rows = current.shape[0]
    mixed = jnp.broadcast_to(taps[CONV], current.shape)
    for offset in range(CONV):
        mixed = mixed + taps[offset] * extended[offset : offset + length_rows].astype(jnp.float32)
    return jax.nn.silu(mixed).astype(jnp.bfloat16)


def join_chain(earlier, later):
    return (earlier[0] + later[0], jnp.exp(later[0])[:, None, None] * earlier[1] + later[1])


def carry_block(state, inputs):
    decay_sum, added = inputs
    return (jnp.exp(decay_sum)[:, None, None] * state + added, state)


def pick_group(values, group):
    shaped = values.reshape(values.shape[:-1] + (N, G))
    return lax.dynamic_index_in_dim(shaped, group, shaped.ndim - 1, keepdims=False)


def on_device(
    tokens,
    project_weight,
    state_weight,
    step_weight,
    mixer_taps,
    state_taps,
    step_bias,
    decay_log,
    norm_gain,
):
    inner_id = lax.axis_index("inner")
    project_rows, state_rows, step_rows = (
        lax.all_gather(project_weight, "ctx", axis=0, tiled=True),
        lax.all_gather(state_weight, "ctx", axis=0, tiled=True),
        lax.all_gather(step_weight, "ctx", axis=0, tiled=True),
    )
    heads_here = step_weight.shape[1]
    width_here = project_weight.shape[2]
    model_width = project_rows.shape[0]
    group = inner_id * heads_here // (H // G)
    full_cols = lax.all_gather(state_rows, "inner", axis=2, tiled=True)
    slice_cols = N
    state_cols = pick_group(full_cols, group)
    state_conv = pick_group(state_taps, group)
    joined = jnp.concatenate(
        [
            project_rows.reshape(model_width, 2 * width_here),
            state_cols.reshape(model_width, 2 * slice_cols),
            step_rows,
        ],
        axis=1,
    )
    projected = jnp.dot(
        lax.all_gather(tokens, "inner", axis=0, tiled=True),
        joined,
        preferred_element_type=jnp.float32,
    ).astype(jnp.bfloat16)
    rows_total = projected.shape[0]
    gate_values = projected[:, :width_here]
    x_pre = projected[:, width_here : 2 * width_here]
    state_pre = projected[:, 2 * width_here : 2 * width_here + 2 * slice_cols].reshape(
        rows_total, 2, slice_cols
    )
    step_raw = projected[:, 2 * width_here + 2 * slice_cols :]
    edge_row = rows_total - (CONV - 1)
    prior_x, prior_state = passed_along((x_pre[edge_row:], state_pre[edge_row:]), "ctx", 1)
    x_vals = conv_apply(mixer_taps, prior_x, x_pre)
    state_vals = conv_apply(state_conv, prior_state, state_pre)
    blocks = rows_total // SPAN
    b_blocks = state_vals[:, 0].reshape(blocks, SPAN, N)
    c_blocks = state_vals[:, 1].reshape(blocks, SPAN, N)
    step_size = jax.nn.softplus(step_raw.astype(jnp.float32) + step_bias)
    step_heads = step_size.T.reshape(heads_here, blocks, SPAN)
    cumul = jnp.cumsum(step_heads * (-jnp.exp(decay_log))[:, None, None], axis=2)
    scores = jnp.einsum("ctn,csn->cts", c_blocks, b_blocks, preferred_element_type=jnp.float32)
    lower = jnp.tril(jnp.ones((SPAN, SPAN), dtype=bool))
    spacing = jnp.where(lower, cumul[..., :, None] - cumul[..., None, :], -jnp.inf)
    mixing = (scores[None] * jnp.exp(spacing) * step_heads[:, :, None, :]).astype(jnp.bfloat16)
    x_blocks = x_vals.reshape(blocks, SPAN, heads_here, P_SIZE)
    diagonal = jnp.einsum("hcts,cshp->cthp", mixing, x_blocks, preferred_element_type=jnp.float32)
    ending = cumul[:, :, -1]
    to_end = jnp.exp(ending[..., None] - cumul) * step_heads
    weighted_b = (b_blocks.astype(jnp.float32)[None] * to_end[..., None]).astype(jnp.bfloat16)
    fresh = jnp.einsum("hcsn,cshp->chnp", weighted_b, x_blocks, preferred_element_type=jnp.float32)
    empty_state = jnp.zeros((heads_here, N, P_SIZE), jnp.float32)
    block_state, local_in = lax.scan(carry_block, empty_state, (ending.T, fresh))
    block_log = jnp.sum(ending, axis=1)
    before_log = (jnp.cumsum(ending, axis=1) - ending).T
    _, prior_block = entering(
        (block_log, block_state), "ctx", join_chain, (jnp.zeros_like(block_log), empty_state)
    )
    state_in = local_in + jnp.exp(before_log)[:, :, None, None] * prior_block[None]
    c_scaled = (c_blocks.astype(jnp.float32)[None] * jnp.exp(cumul)[..., None]).astype(jnp.bfloat16)
    state_high = state_in.astype(jnp.bfloat16)
    state_low = (state_in - state_high.astype(jnp.float32)).astype(jnp.bfloat16)
    offdiag = jnp.einsum(
        "hctn,chnp->cthp", c_scaled, state_high, preferred_element_type=jnp.float32
    )
    offdiag = offdiag + jnp.einsum(
        "hctn,chnp->cthp", c_scaled, state_low, preferred_element_type=jnp.float32
    )
    outputs = (diagonal + offdiag).reshape(rows_total, width_here)
    gated = (outputs * jax.nn.silu(gate_values.astype(jnp.float32))).astype(jnp.bfloat16)
    gated_wide = gated.astype(jnp.float32)
    squares = jnp.sum(gated_wide * gated_wide, axis=1)
    group_devices = H // G // heads_here
    for bit in range(group_devices.bit_length() - 1):
        squares = squares + partner(squares, "inner", bit)
    power = squares[:, None] / (H * P_SIZE // G)
    gain_here = lax.dynamic_slice_in_dim(norm_gain, inner_id * width_here, width_here, 0)
    normed = (gated_wide * lax.rsqrt(power + EPSILON) * gain_here).astype(jnp.bfloat16)
    result = lax.all_to_all(normed, "inner", split_axis=0, concat_axis=1, tiled=True)
    return result


def solution(mesh):
    placed = (
        P(("ctx", "inner"), None),
        P("ctx", None, "inner"),
        P("ctx", None, "inner"),
        P("ctx", "inner"),
        P(None, "inner"),
        P(),
        P("inner"),
        P("inner"),
        P(),
    )
    return jax.shard_map(
        on_device, mesh=mesh, in_specs=placed, out_specs=P(("ctx", "inner"), None), check_vma=False
    )
```

profile of v0, /device:TPU:480, one launch (start us, length us, event | category | flops | bytes accessed | tf_op | source)
XLA Modules:
  0.0 455.8 jit_solution(17512234280697024061)
XLA Ops:
  8.1 30.7 %all_gather.26 = bf16[2048,2,32]{2,1,0:T(2,128)(2,1)S(1)} all-gather(bf16[64,2,32]{2,1,0:T(2,128)(2,1)S(1)} %copy.91), channel_id=1, replica_groups=mesh['ctx'=32,'inner'=16] {'ctx'}, dimensions={0}, use_global_device_ids=true | all-gather | bytes 270336 | tf_op jit(solution)/shard_map/all_gather | solution.py:84
  38.8 1.8 copy.92
  41.4 29.1 %all-gather.2 = bf16[32,64,4]{1,2,0:T(4,128)(2,1)S(1)} all-gather(bf16[1,64,4]{1,2,0:T(4,128)(2,1)S(1)} %bitcast.102), channel_id=1, replica_groups=mesh['ctx'=32,'inner'=16] {'ctx'}, dimensions={0}, use_global_device_ids=true | all-gather | bytes 16896 | tf_op jit(solution)/shard_map/all_gather | solution.py:85
  72.8 6.1 %all-gather.8.cloned.1.call-done = bf16[2048,2,256]{2,1,0:T(2,128)(2,1)} async-done(((bf16[64,2,256]{2,1,0:T(2,128)(2,1)}), bf16[2048,2,256]{2,1,0:T(2,128)(2,1)}) %all-gather.8.cloned.1.call-update) | async-done | bytes 2097168 | tf_op jit(solution)/shard_map/all_gather | solution.py:83
  78.9 2.0 copy.123
  81.0 66.3 %all-gather.10.cloned.1.call-done = bf16[2048,2,512]{0,1,2:T(2,128)(2,1)} async-done(((bf16[2048,2,32]{0,1,2:T(2,128)(2,1)}), bf16[2048,2,512]{0,1,2:T(2,128)(2,1)}) %all-gather.10.cloned.1.call-update) | async-done | bytes 4194320 | tf_op jit(solution)/shard_map/all_gather | solution.py:91
  147.3 1.9 constant_dynamic-slice_fusion.2
  149.6 1.3 copy.95
  150.9 85.3 %all-gather.12.cloned.1.call-done = bf16[2048,2048]{1,0:T(8,128)(2,1)} async-done(((bf16[128,2048]{1,0:T(8,128)(2,1)}), bf16[2048,2048]{1,0:T(8,128)(2,1)}) %all-gather.12.cloned.1.call-update) | async-done | bytes 8388624 | tf_op jit(solution)/shard_map/all_gather | solution.py:104
  236.1 10.8 %fusion.12 = bf16[2048,772]{0,1:T(8,128)(2,1)S(1)} fusion(bf16[2048,2048]{1,0:T(8,128)(2,1)} %all-gather.12.cloned.1.call-done, bf16[2048,4]{1,0:T(8,128)(2,1)} %bitcast.92, bf16[2048,256]{1,0:T(8,128)(2,1)} %copy.95, bf16[2048,512]{1,0:T(8,128)(2,1)S(1)} %bitcast.91), kind=kOutput, calls=%fused_computation.21 | convolution fusion | flops 6487072768 | bytes 14712832 | tf_op jit(solution)/shard_map/dot_general | solution.py:103
  247.2 1.4 copy-done.1
  250.2 1.9 collective-permute-start
  252.2 2.1 collective-permute-start.1
  254.4 1.4 collective-permute-done
  255.7 2.2 fusion.51
  258.2 2.2 multiply_convert_fusion.7
  260.8 3.9 fusion.26
  264.7 28.8 %while.26 = (s32[]{:T(128)}, f32[4,128,64]{2,1,0:T(8,128)S(1)}, f32[16,4,128,64]{3,2,1,0:T(8,128)}, f32[16,4]{1,0:T(8,128)S(1)}, f32[16,4,128,64]{3,2,1,0:T(8,128)}, /*index=5*/s32[]{:T(128)}, s32[]{:T(128)}) while((s32[]{:T(128)}, f32[4,128,64]{2,1,0:T(8,128)S(1)}, f32[16,4,128,64]{3,2,1,0:T(8,128)}, f32[16,4]{1,0:T(8,128)S(1)}, ...), condition=%wide.region_2.3_spmd.clone, body=%wide.region_1.2_spmd.clone.sunk | while | flops 131075 | bytes 787088 | solution.py:136
  294.4 1.3 dynamic-slice
  296.8 42.4 %all-reduce = bf16[128]{0:T(256)(128)(2,1)S(1)} all-reduce(bf16[128]{0:T(256)(128)(2,1)S(1)} %dynamic-update-slice), channel_id=2, replica_groups=mesh['ctx'=32,'inner'=16] {'ctx'}, use_global_device_ids=true, to_apply=%add | all-reduce | flops 128 | bytes 512
  340.3 3.3 fusion.18
  343.6 22.2 %all-gather.14.cloned.1.call-done = bf16[128,128,64]{1,2,0:T(8,128)(2,1)} async-done(((bf16[4,128,64]{1,2,0:T(8,128)(2,1)}), bf16[128,128,64]{1,2,0:T(8,128)(2,1)}) %all-gather.14.cloned.1.call-update) | async-done | bytes 2097168 | tf_op jit(solution)/shard_map/all_gather | solution.py:24
  365.8 34.4 %while.25 = (s32[]{:T(128)}, f32[4,128,64]{2,1,0:T(8,128)S(1)}, s32[]{:T(128)}, bf16[32,4]{1,0:T(8,128)(2,1)S(1)}, bf16[32,4,128,64]{2,3,1,0:T(8,128)(2,1)}, /*index=5*/s32[]{:T(128)}, s32[]{:T(128)}, s32[]{:T(128)}) while((s32[]{:T(128)}, f32[4,128,64]{2,1,0:T(8,128)S(1)}, s32[]{:T(128)}, bf16[32,4]{1,0:T(8,128)(2,1)S(1)}, ...), condition=%wide.region_6.7_spmd, body=%wide.region_5.6_spmd.sunk | while | flops 98313 | bytes 589991 | solution.py:38
  400.2 5.2 %fusion.15 = f32[16,4,64,128]{3,2,1,0:T(8,128)S(1)} fusion(f32[16,4,128,64]{3,2,1,0:T(8,128)} %get-tuple-element.77, f32[4,16,128]{2,0,1:T(4,128)S(1)} %copy.110, f32[16,128,128]{2,1,0:T(8,128)S(1)} %convert_element_type.135, f32[4,128,64]{2,1,0:T(8,128)S(1)} %get-tuple-element.79, f32[16,4]{1,0:T(8,128)S(1)} %copy.107), kind=kOutput, calls=%fused_computation.22 | convolution fusion | flops 139460608 | bytes 5406976 | tf_op jit(solution)/shard_map/hctn,chnp->cthp/dot_general | solution.py:149
  405.5 2.7 add_bitcast_fusion
  409.4 2.4 fusion.23
  411.8 3.4 collective-permute-start.2
  415.2 2.2 collective-permute-done.2
  417.4 4.9 %collective-permute-start.3 = (f32[2048]{0:T(1024)S(1)}, f32[2048]{0:T(1024)S(1)}, u32[]{:S(2)}, u32[]{:S(2)}) collective-permute-start(f32[2048]{0:T(1024)S(1)} %add.124), channel_id=1, source_target_pairs={{0,2},{1,3},{2,0},{3,1},{4,6},{5,7},{6,4},{7,5},{8,10},{9,11},{10,... | collective-permute-start | bytes 24584 | tf_op jit(solution)/shard_map/ppermute | solution.py:44
  423.0 1.4 collective-permute-done.3
  424.8 23.1 %all_to_all.19 = bf16[16,128,256]{1,2,0:T(8,128)(2,1)S(1)} all-to-all(bf16[16,128,256]{1,2,0:T(8,128)(2,1)S(1)} %copy_bitcast_fusion), channel_id=1, replica_groups=mesh['ctx'=32,'inner'=16] {'inner'}, dimensions={0} | all-to-all | bytes 2097152 | tf_op jit(solution)/shard_map/all_to_all | solution.py:162
  448.0 1.3 copy.115
  (233 shorter events, 73.9 us)
Async XLA Ops:
  6.5 34.9 %copy-start.5 = (bf16[64,4]{0,1:T(4,128)(2,1)S(1)}, bf16[64,4]{0,1:T(4,128)(2,1)}, u32[]{:S(2)}) copy-start(bf16[64,4]{0,1:T(4,128)(2,1)} %param.16) | copy-start | bytes 1540
  6.5 65.1 %copy-start.3 = (f32[5,2,512]{2,1,0:T(2,128)S(1)}, f32[5,2,512]{2,1,0:T(2,128)}, u32[]{:S(2)}) copy-start(f32[5,2,512]{2,1,0:T(2,128)} %param.18) | copy-start | bytes 61444
  6.5 72.4 %all-gather.8.cloned.1.call-start = ((), (), s32[]{:S(2)}) async-start(), calls=%async_computation.1 | async-start | bytes 2162688 | tf_op jit(solution)/shard_map/all_gather | solution.py:83
  7.3 140.0 %all-gather.10.cloned.1.call-start = ((), (), s32[]{:S(2)}) async-start(), calls=%async_computation.2 | async-start | bytes 4456448 | tf_op jit(solution)/shard_map/all_gather | solution.py:91
  38.8 34.0 %copy-start.7 = (f32[4]{0:T(128)S(1)}, f32[4]{0:T(128)}, u32[]{:S(2)}) copy-start(f32[4]{0:T(128)} %param.20) | copy-start | bytes 52
  38.8 34.0 %copy-start.4 = (f32[5,256]{1,0:T(8,128)S(1)}, f32[5,256]{1,0:T(8,128)}, u32[]{:S(2)}) copy-start(f32[5,256]{1,0:T(8,128)} %param.17) | copy-start | bytes 15364
  40.6 195.5 %all-gather.12.cloned.1.call-start = ((), (), s32[]{:S(2)}) async-start(), calls=%async_computation.3 | async-start | bytes 8912896 | tf_op jit(solution)/shard_map/all_gather | solution.py:104
  41.3 324.5 %all-gather.14.cloned.1.call-start = ((), (), s32[]{:S(2)}) async-start(), calls=%async_computation.4 | async-start | bytes 2162688 | tf_op jit(solution)/shard_map/all_gather | solution.py:24
  246.9 1.7 copy-start.1
  247.0 1.7 copy-start.6
  250.2 5.6 %collective-permute-start = (bf16[3,256]{0,1:T(8,128)(2,1)S(1)}, bf16[3,256]{0,1:T(8,128)(2,1)S(1)}, u32[]{:S(2)}, u32[]{:S(2)}) collective-permute-start(bf16[3,256]{0,1:T(8,128)(2,1)S(1)} %get-tuple-element.164), channel_id=1, source_target_pairs={{0,16},{16,32},{32,48},{48,64},{64,80},{80,96},{96,112},{112,128},... | collective-permute-start | bytes 4616 | tf_op jit(solution)/shard_map/ppermute | solution.py:18
  252.2 5.9 %collective-permute-start.1 = (bf16[3,2,128]{0,2,1:T(8,128)(2,1)S(1)}, bf16[3,2,128]{0,2,1:T(8,128)(2,1)S(1)}, u32[]{:S(2)}, u32[]{:S(2)}) collective-permute-start(bf16[3,2,128]{0,2,1:T(8,128)(2,1)S(1)} %bitcast.94), channel_id=1, source_target_pairs={{0,16},{16,32},{32,48},{48,64},{64,80},{80,96},{96,112},{112,128},... | collective-permute-start | bytes 4616 | tf_op jit(solution)/shard_map/ppermute | solution.py:18
  400.2 5.2 %copy-start = (f32[16,4,128,64]{3,2,1,0:T(8,128)S(1)}, f32[16,4,128,64]{3,2,1,0:T(8,128)}, u32[]{:S(2)}) copy-start(f32[16,4,128,64]{3,2,1,0:T(8,128)} %get-tuple-element.77) | copy-start | bytes 6291460
  400.2 5.2 %copy-start.2 = (f32[16,4,64,128]{3,2,1,0:T(8,128)S(1)}, f32[16,4,64,128]{3,2,1,0:T(8,128)}, u32[]{:S(2)}) copy-start(f32[16,4,64,128]{3,2,1,0:T(8,128)} %fusion.18) | copy-start | bytes 6291460
  411.8 5.5 %collective-permute-start.2 = (f32[2048]{0:T(1024)S(1)}, f32[2048]{0:T(1024)S(1)}, u32[]{:S(2)}, u32[]{:S(2)}) collective-permute-start(f32[2048]{0:T(1024)S(1)} %get-tuple-element.160), channel_id=1, source_target_pairs={{0,1},{1,0},{2,3},{3,2},{4,5},{5,4},{6,7},{7,6},{8,9},{9,8},{10,11... | collective-permute-start | bytes 24584 | tf_op jit(solution)/shard_map/ppermute | solution.py:44
  417.4 7.0 %collective-permute-start.3 = (f32[2048]{0:T(1024)S(1)}, f32[2048]{0:T(1024)S(1)}, u32[]{:S(2)}, u32[]{:S(2)}) collective-permute-start(f32[2048]{0:T(1024)S(1)} %add.124), channel_id=1, source_target_pairs={{0,2},{1,3},{2,0},{3,1},{4,6},{5,7},{6,4},{7,5},{8,10},{9,11},{10,... | collective-permute-start | bytes 24584 | tf_op jit(solution)/shard_map/ppermute | solution.py:44
Sparse Core Ops, SparseCore 0:
  9.5 69.3 all-gather.7
  81.9 65.2 all-gather.9
  150.3 85.8 all-gather.11
  294.5 71.2 all-gather.13
where the time goes:
time: 458 us; the launch traced here: 456 us
  waiting for transfers between devices  186 us (41%)
  blocking collectives  125 us (27%)
  local copies, waits for them, and re-layouts  48.5 us (11%)
  other arithmetic  41.3 us (9%)
  matrix products  26.4 us (6%)
  between operations  14.2 us (3%)
  starting transfers between devices  12.4 us (3%)
    all_gather x1, waiting for transfers between devices, on_device(): lax.all_gather(tokens, 'inner', axis=0, tiled=True)  85.3 us
    all_gather x1, waiting for transfers between devices, on_device(): full_cols = lax.all_gather(state_rows, 'inner', axis=2, tiled=True)  66.3 us
    unnamed x1, blocking collectives  42.4 us
    all_gather x1, blocking collectives, on_device(): lax.all_gather(state_weight, 'ctx', axis=0, tiled=True)  30.7 us
    dynamic_slice x60, local copies, waits for them, and re-layouts, one(): lax.dynamic_index_in_dim(a, turn, 0, False).astype(own.dtype)  29.4 us
    all_gather x1, blocking collectives, on_device(): lax.all_gather(step_weight, 'ctx', axis=0, tiled=True)  29.1 us
    all_to_all x1, blocking collectives, on_device(): lax.all_to_all(normed, 'inner', split_axis=0, concat_axis=1, tiled=True)  23.1 us
    all_gather x1, waiting for transfers between devices, entering(): lax.all_gather(a.astype(kind), axis)  22.2 us
  transfers between devices with their start and end apart: 8, of which 7 were waited for; matrix products, arithmetic and copies ran while one was open for 4% of the time, Pallas kernels for 0%

commit v1 on v0

--- a/solution.py
+++ b/solution.py
@@ -88,7 +88,14 @@
     width_here = project_weight.shape[2]
     model_width = project_rows.shape[0]
     group = inner_id * heads_here // (H // G)
-    full_cols = lax.all_gather(state_rows, "inner", axis=2, tiled=True)
+    ring = [state_rows]
+    for hop in range(15):
+        ring.append(lax.ppermute(ring[-1], "inner", [(dev, (dev + 1) % 16) for dev in range(16)]))
+    full_cols = jnp.roll(
+        jnp.concatenate(ring[::-1], axis=2),
+        (lax.axis_index("inner") + 1) * ring[0].shape[2],
+        axis=2,
+    )
     slice_cols = N
     state_cols = pick_group(full_cols, group)
     state_conv = pick_group(state_taps, group)

time: 458 us -> 719 us (1.57)
  local copies, waits for them, and re-layouts: 48.5 us -> 264 us
  starting transfers between devices: 12.4 us -> 43.3 us
    ppermute x0 -> x15, waiting for transfers between devices: none -> 165 us  [on_device(): lax.ppermute(ring[-1], 'inner', [(dev, (dev + 1) % 16) for dev in range(1...]
    concatenate x0 -> x1, local copies, waits for them, and re-layouts: none -> 135 us  [on_device(): jnp.roll(jnp.concatenate(ring[::-1], axis=2), (lax.axis_index('inner') +...]
    all_gather x1, waiting for transfers between devices: 85.3 us -> 0.02 us  [on_device(): lax.all_gather(tokens, 'inner', axis=0, tiled=True)]
    all_gather x1 -> x0, waiting for transfers between devices: 66.3 us -> none  [on_device(): full_cols = lax.all_gather(state_rows, 'inner', axis=2, tiled=True)]
    ppermute x0 -> x15, local copies, waits for them, and re-layouts: none -> 47.5 us  [on_device(): lax.ppermute(ring[-1], 'inner', [(dev, (dev + 1) % 16) for dev in range(1...]
    ppermute x0 -> x15, starting transfers between devices: none -> 30.8 us  [on_device(): lax.ppermute(ring[-1], 'inner', [(dev, (dev + 1) % 16) for dev in range(1...]
    dynamic_slice x0 -> x2, local copies, waits for them, and re-layouts: none -> 26.9 us  [on_device(): jnp.roll(jnp.concatenate(ring[::-1], axis=2), (lax.axis_index('inner') +...]
  transfers between devices with their start and end apart: 8 -> 22, of which waited for: 7 -> 18; matrix products, arithmetic and copies ran while one was open for 4% -> 32% of each run, Pallas kernels for 0% -> 0%
where the time goes in v1:
time: 719 us; the launch traced here: 711 us
  local copies, waits for them, and re-layouts  264 us (37%)
  waiting for transfers between devices  192 us (27%)
  blocking collectives  126 us (18%)
  starting transfers between devices  43.3 us (6%)
  other arithmetic  42.9 us (6%)
  matrix products  26.1 us (4%)
  between operations  14.5 us (2%)
    ppermute x15, waiting for transfers between devices, on_device(): lax.ppermute(ring[-1], 'inner', [(dev, (dev + 1) % 16) for dev in range(1...  165 us
    concatenate x1, local copies, waits for them, and re-layouts, on_device(): jnp.roll(jnp.concatenate(ring[::-1], axis=2), (lax.axis_index('inner') +...  135 us
    ppermute x15, local copies, waits for them, and re-layouts, on_device(): lax.ppermute(ring[-1], 'inner', [(dev, (dev + 1) % 16) for dev in range(1...  47.5 us
    unnamed x1, blocking collectives  44 us
    ppermute x15, starting transfers between devices, on_device(): lax.ppermute(ring[-1], 'inner', [(dev, (dev + 1) % 16) for dev in range(1...  30.8 us
    all_gather x1, blocking collectives, on_device(): lax.all_gather(state_weight, 'ctx', axis=0, tiled=True)  30 us
    all_gather x1, blocking collectives, on_device(): lax.all_gather(step_weight, 'ctx', axis=0, tiled=True)  29.4 us
    dynamic_slice x60, local copies, waits for them, and re-layouts, one(): lax.dynamic_index_in_dim(a, turn, 0, False).astype(own.dtype)  29.4 us
  transfers between devices with their start and end apart: 22, of which 18 were waited for; matrix products, arithmetic and copies ran while one was open for 32% of the time, Pallas kernels for 0%

profile of v1, /device:TPU:480, one launch (start us, length us, event | category | flops | bytes accessed | tf_op | source)
XLA Modules:
  0.0 710.8 jit_solution(13747331429049006565)
XLA Ops:
  8.9 30.0 %all_gather.23 = bf16[2048,2,32]{2,1,0:T(2,128)(2,1)S(1)} all-gather(bf16[64,2,32]{2,1,0:T(2,128)(2,1)S(1)} %copy.116), channel_id=1, replica_groups=mesh['ctx'=32,'inner'=16] {'ctx'}, dimensions={0}, use_global_device_ids=true | all-gather | bytes 270336 | tf_op jit(solution)/shard_map/all_gather | solution.py:84
  39.5 4.1 collective-permute-start
  43.6 10.7 %collective-permute-done = bf16[2048,2,32]{0,2,1:T(8,128)(2,1)S(1)} collective-permute-done((bf16[2048,2,32]{0,2,1:T(8,128)(2,1)S(1)}, bf16[2048,2,32]{0,2,1:T(8,128)(2,1)S(1)}, u32[]{:S(2)}, u32[]{:S(2)}) %collective-permute-start) | collective-permute-done | bytes 262176 | tf_op jit(solution)/shard_map/ppermute | solution.py:93
  56.3 11.3 %collective-permute-done.1 = bf16[2048,2,32]{0,2,1:T(8,128)(2,1)S(1)} collective-permute-done((bf16[2048,2,32]{0,2,1:T(8,128)(2,1)S(1)}, bf16[2048,2,32]{0,2,1:T(8,128)(2,1)S(1)}, u32[]{:S(2)}, u32[]{:S(2)}) %collective-permute-start.1) | collective-permute-done | bytes 262176 | tf_op jit(solution)/shard_map/ppermute | solution.py:93
  69.5 10.4 %collective-permute-done.2 = bf16[2048,2,32]{0,2,1:T(8,128)(2,1)S(1)} collective-permute-done((bf16[2048,2,32]{0,2,1:T(8,128)(2,1)S(1)}, bf16[2048,2,32]{0,2,1:T(8,128)(2,1)S(1)}, u32[]{:S(2)}, u32[]{:S(2)}) %collective-permute-start.2) | collective-permute-done | bytes 262176 | tf_op jit(solution)/shard_map/ppermute | solution.py:93
  81.8 9.7 %collective-permute-done.3 = bf16[2048,2,32]{0,2,1:T(8,128)(2,1)S(1)} collective-permute-done((bf16[2048,2,32]{0,2,1:T(8,128)(2,1)S(1)}, bf16[2048,2,32]{0,2,1:T(8,128)(2,1)S(1)}, u32[]{:S(2)}, u32[]{:S(2)}) %collective-permute-start.3) | collective-permute-done | bytes 262176 | tf_op jit(solution)/shard_map/ppermute | solution.py:93
  93.3 9.7 %collective-permute-done.4 = bf16[2048,2,32]{0,2,1:T(8,128)(2,1)S(1)} collective-permute-done((bf16[2048,2,32]{0,2,1:T(8,128)(2,1)S(1)}, bf16[2048,2,32]{0,2,1:T(8,128)(2,1)S(1)}, u32[]{:S(2)}, u32[]{:S(2)}) %collective-permute-start.4) | collective-permute-done | bytes 262176 | tf_op jit(solution)/shard_map/ppermute | solution.py:93
  105.0 13.2 %collective-permute-done.5 = bf16[2048,2,32]{0,2,1:T(8,128)(2,1)S(1)} collective-permute-done((bf16[2048,2,32]{0,2,1:T(8,128)(2,1)S(1)}, bf16[2048,2,32]{0,2,1:T(8,128)(2,1)S(1)}, u32[]{:S(2)}, u32[]{:S(2)}) %collective-permute-start.5) | collective-permute-done | bytes 262176 | tf_op jit(solution)/shard_map/ppermute | solution.py:93
  120.8 9.7 %collective-permute-done.6 = bf16[2048,2,32]{0,2,1:T(8,128)(2,1)S(1)} collective-permute-done((bf16[2048,2,32]{0,2,1:T(8,128)(2,1)S(1)}, bf16[2048,2,32]{0,2,1:T(8,128)(2,1)S(1)}, u32[]{:S(2)}, u32[]{:S(2)}) %collective-permute-start.6) | collective-permute-done | bytes 262176 | tf_op jit(solution)/shard_map/ppermute | solution.py:93
  133.1 15.9 %collective-permute-done.7 = bf16[2048,2,32]{0,2,1:T(8,128)(2,1)S(1)} collective-permute-done((bf16[2048,2,32]{0,2,1:T(8,128)(2,1)S(1)}, bf16[2048,2,32]{0,2,1:T(8,128)(2,1)S(1)}, u32[]{:S(2)}, u32[]{:S(2)}) %collective-permute-start.7) | collective-permute-done | bytes 262176 | tf_op jit(solution)/shard_map/ppermute | solution.py:93
  151.6 15.6 %collective-permute-done.8 = bf16[2048,2,32]{0,2,1:T(8,128)(2,1)S(1)} collective-permute-done((bf16[2048,2,32]{0,2,1:T(8,128)(2,1)S(1)}, bf16[2048,2,32]{0,2,1:T(8,128)(2,1)S(1)}, u32[]{:S(2)}, u32[]{:S(2)}) %collective-permute-start.8) | collective-permute-done | bytes 262176 | tf_op jit(solution)/shard_map/ppermute | solution.py:93
  169.7 15.3 %collective-permute-done.9 = bf16[2048,2,32]{0,2,1:T(8,128)(2,1)S(1)} collective-permute-done((bf16[2048,2,32]{0,2,1:T(8,128)(2,1)S(1)}, bf16[2048,2,32]{0,2,1:T(8,128)(2,1)S(1)}, u32[]{:S(2)}, u32[]{:S(2)}) %collective-permute-start.9) | collective-permute-done | bytes 262176 | tf_op jit(solution)/shard_map/ppermute | solution.py:93
  187.7 9.7 %collective-permute-done.10 = bf16[2048,2,32]{0,2,1:T(8,128)(2,1)S(1)} collective-permute-done((bf16[2048,2,32]{0,2,1:T(8,128)(2,1)S(1)}, bf16[2048,2,32]{0,2,1:T(8,128)(2,1)S(1)}, u32[]{:S(2)}, u32[]{:S(2)}) %collective-permute-start.10) | collective-permute-done | bytes 262176 | tf_op jit(solution)/shard_map/ppermute | solution.py:93
  199.9 10.7 %collective-permute-done.11 = bf16[2048,2,32]{0,2,1:T(8,128)(2,1)S(1)} collective-permute-done((bf16[2048,2,32]{0,2,1:T(8,128)(2,1)S(1)}, bf16[2048,2,32]{0,2,1:T(8,128)(2,1)S(1)}, u32[]{:S(2)}, u32[]{:S(2)}) %collective-permute-start.11) | collective-permute-done | bytes 262176 | tf_op jit(solution)/shard_map/ppermute | solution.py:93
  213.3 12.0 %collective-permute-done.12 = bf16[2048,2,32]{0,2,1:T(8,128)(2,1)S(1)} collective-permute-done((bf16[2048,2,32]{0,2,1:T(8,128)(2,1)S(1)}, bf16[2048,2,32]{0,2,1:T(8,128)(2,1)S(1)}, u32[]{:S(2)}, u32[]{:S(2)}) %collective-permute-start.12) | collective-permute-done | bytes 262176 | tf_op jit(solution)/shard_map/ppermute | solution.py:93
  227.9 11.6 %collective-permute-done.13 = bf16[2048,2,32]{0,2,1:T(8,128)(2,1)} collective-permute-done((bf16[2048,2,32]{0,2,1:T(8,128)(2,1)S(1)}, bf16[2048,2,32]{0,2,1:T(8,128)(2,1)}, u32[]{:S(2)}, u32[]{:S(2)}) %collective-permute-start.13) | collective-permute-done | bytes 262176 | tf_op jit(solution)/shard_map/ppermute | solution.py:93
  241.4 29.4 %all-gather.2 = bf16[32,64,4]{1,2,0:T(4,128)(2,1)S(1)} all-gather(bf16[1,64,4]{1,2,0:T(4,128)(2,1)S(1)} %bitcast.101), channel_id=1, replica_groups=mesh['ctx'=32,'inner'=16] {'ctx'}, dimensions={0}, use_global_device_ids=true | all-gather | bytes 16896 | tf_op jit(solution)/shard_map/all_gather | solution.py:85
  276.7 3.5 copy.130
  280.1 3.4 copy.129
  297.3 3.5 copy.124
  321.2 134.7 %concatenate.15 = bf16[2048,2,1024]{2,1,0:T(2,128)(2,1)} concatenate(bf16[2048,2,32]{2,1,0:T(2,128)(2,1)} %copy.118, bf16[2048,2,32]{2,1,0:T(2,128)(2,1)} %copy.119, bf16[2048,2,32]{2,1,0:T(2,128)(2,1)} %copy.120, bf16[2048,2,32]{2,1,0:T(2,128)(2,1)} %copy.121, bf16[2048,2,32]{2,1,0:T(2,128)(2,1)} %copy.122, bf16[2048,2,32]{2,1,0:T(2,128)(2,1)} %copy.123, ...), dimensions={2} | concatenate | bytes 16777216 | tf_op jit(solution)/shard_map/jit(_roll_dynamic)/concatenate | solution.py:94
  456.0 11.0 %constant_dynamic-slice_fusion.3 = bf16[2048,2,512]{2,1,0:T(2,128)(2,1)} fusion(bf16[2048,2,1024]{2,1,0:T(2,128)(2,1)} %concatenate.15, s32[]{:T(128)S(6)} %select_n.44), kind=kLoop, calls=%fused_computation.86 | loop fusion | bytes 8388612 | tf_op jit(solution)/shard_map/jit(_roll_dynamic)/dynamic_slice | solution.py:94
  466.9 15.9 %copy.148 = bf16[2048,2,512]{0,1,2:T(2,128)(2,1)} copy(bf16[2048,2,512]{2,1,0:T(2,128)(2,1)} %constant_dynamic-slice_fusion.3) | data formatting | bytes 8388608 | tf_op jit(solution)/shard_map/jit(_roll_dynamic)/dynamic_slice | solution.py:94
  487.8 10.4 %fusion.12 = bf16[2048,772]{0,1:T(8,128)(2,1)S(1)} fusion(bf16[2048,2048]{1,0:T(8,128)(2,1)} %all-gather.9.cloned.1.call-done, bf16[2048,4]{1,0:T(8,128)(2,1)} %bitcast.93, bf16[2048,256]{1,0:T(8,128)(2,1)S(1)} %copy.151, bf16[2048,512]{1,0:T(8,128)(2,1)S(1)} %bitcast.92), kind=kOutput, calls=%fused_computation.21 | convolution fusion | flops 6487072768 | bytes 14712832 | tf_op jit(solution)/shard_map/dot_general | solution.py:110
  515.3 4.0 fusion.26
  519.3 28.7 %while.26 = (s32[]{:T(128)}, f32[4,128,64]{2,1,0:T(8,128)S(1)}, f32[16,4,128,64]{3,2,1,0:T(8,128)}, f32[16,4]{1,0:T(8,128)S(1)}, f32[16,4,128,64]{3,2,1,0:T(8,128)}, /*index=5*/s32[]{:T(128)}, s32[]{:T(128)}) while((s32[]{:T(128)}, f32[4,128,64]{2,1,0:T(8,128)S(1)}, f32[16,4,128,64]{3,2,1,0:T(8,128)}, f32[16,4]{1,0:T(8,128)S(1)}, ...), condition=%wide.region_2.3_spmd.clone, body=%wide.region_1.2_spmd.clone.sunk | while | flops 131075 | bytes 787088 | solution.py:143
  551.4 44.0 %all-reduce = bf16[128]{0:T(256)(128)(2,1)S(1)} all-reduce(bf16[128]{0:T(256)(128)(2,1)S(1)} %dynamic-update-slice), channel_id=2, replica_groups=mesh['ctx'=32,'inner'=16] {'ctx'}, use_global_device_ids=true, to_apply=%add | all-reduce | flops 128 | bytes 512
  600.5 20.4 %all-gather.11.cloned.1.call-done = bf16[128,128,64]{1,2,0:T(8,128)(2,1)} async-done(((bf16[4,128,64]{1,2,0:T(8,128)(2,1)}), bf16[128,128,64]{1,2,0:T(8,128)(2,1)}) %all-gather.11.cloned.1.call-update) | async-done | bytes 2097168 | tf_op jit(solution)/shard_map/all_gather | solution.py:24
  621.0 34.3 %while.25 = (s32[]{:T(128)}, f32[4,128,64]{2,1,0:T(8,128)S(1)}, s32[]{:T(128)}, bf16[32,4]{1,0:T(8,128)(2,1)S(1)}, bf16[32,4,128,64]{2,3,1,0:T(8,128)(2,1)}, /*index=5*/s32[]{:T(128)}, s32[]{:T(128)}, s32[]{:T(128)}) while((s32[]{:T(128)}, f32[4,128,64]{2,1,0:T(8,128)S(1)}, s32[]{:T(128)}, bf16[32,4]{1,0:T(8,128)(2,1)S(1)}, ...), condition=%wide.region_6.7_spmd, body=%wide.region_5.6_spmd.sunk | while | flops 98313 | bytes 589991 | solution.py:38
  655.4 5.2 fusion.15
  672.5 4.8 collective-permute-start.18
  679.9 23.0 %all_to_all.19 = bf16[16,128,256]{1,2,0:T(8,128)(2,1)S(1)} all-to-all(bf16[16,128,256]{1,2,0:T(8,128)(2,1)S(1)} %copy_bitcast_fusion), channel_id=1, replica_groups=mesh['ctx'=32,'inner'=16] {'inner'}, dimensions={0} | all-to-all | bytes 2097152 | tf_op jit(solution)/shard_map/all_to_all | solution.py:169
  (326 shorter events, 182.2 us)
Async XLA Ops:
  6.5 234.8 %copy-start.31 = (f32[4]{0:T(128)S(1)}, f32[4]{0:T(128)}, u32[]{:S(2)}) copy-start(f32[4]{0:T(128)} %param.20) | copy-start | bytes 52
  6.5 234.9 %copy-start.28 = (bf16[64,4]{0,1:T(4,128)(2,1)S(1)}, bf16[64,4]{0,1:T(4,128)(2,1)}, u32[]{:S(2)}) copy-start(bf16[64,4]{0,1:T(4,128)(2,1)} %param.16) | copy-start | bytes 1540
  6.5 265.4 %copy-start.22 = (f32[5,2,512]{2,1,0:T(2,128)S(1)}, f32[5,2,512]{2,1,0:T(2,128)}, u32[]{:S(2)}) copy-start(f32[5,2,512]{2,1,0:T(2,128)} %param.18) | copy-start | bytes 61444
  6.5 479.2 %all-gather.7.cloned.1.call-start = ((), (), s32[]{:S(2)}) async-start(), calls=%async_computation.1 | async-start | bytes 2162688 | tf_op jit(solution)/shard_map/all_gather | solution.py:83
  7.3 480.5 %all-gather.9.cloned.1.call-start = ((), (), s32[]{:S(2)}) async-start(), calls=%async_computation.2 | async-start | bytes 8912896 | tf_op jit(solution)/shard_map/all_gather | solution.py:111
  8.0 612.9 %all-gather.11.cloned.1.call-start = ((), (), s32[]{:S(2)}) async-start(), calls=%async_computation.3 | async-start | bytes 2162688 | tf_op jit(solution)/shard_map/all_gather | solution.py:24
  8.9 264.8 %copy-start.27 = (f32[5,256]{1,0:T(8,128)S(1)}, f32[5,256]{1,0:T(8,128)}, u32[]{:S(2)}) copy-start(f32[5,256]{1,0:T(8,128)} %param.17) | copy-start | bytes 15364
  39.5 14.8 %collective-permute-start = (bf16[2048,2,32]{0,2,1:T(8,128)(2,1)S(1)}, bf16[2048,2,32]{0,2,1:T(8,128)(2,1)S(1)}, u32[]{:S(2)}, u32[]{:S(2)}) collective-permute-start(bf16[2048,2,32]{0,2,1:T(8,128)(2,1)S(1)} %copy.117), channel_id=1, source_target_pairs={{0,1},{1,2},{2,3},{3,4},{4,5},{5,6},{6,7},{7,8},{8,9},{9,10},{10,1... | collective-permute-start | bytes 786440 | tf_op jit(solution)/shard_map/ppermute | solution.py:93
  54.4 13.2 %collective-permute-start.1 = (bf16[2048,2,32]{0,2,1:T(8,128)(2,1)S(1)}, bf16[2048,2,32]{0,2,1:T(8,128)(2,1)S(1)}, u32[]{:S(2)}, u32[]{:S(2)}) collective-permute-start(bf16[2048,2,32]{0,2,1:T(8,128)(2,1)S(1)} %collective-permute-done), channel_id=1, source_target_pairs={{0,1},{1,2},{2,3},{3,4},{4,5},{5,6},{6,7},{7,8},{8,9},{9,10},{10,1... | collective-permute-start | bytes 786440 | tf_op jit(solution)/shard_map/ppermute | solution.py:93
  67.5 203.3 %copy-start.7 = (bf16[2048,2,32]{0,2,1:T(8,128)(2,1)}, bf16[2048,2,32]{0,2,1:T(8,128)(2,1)S(1)}, u32[]{:S(2)}) copy-start(bf16[2048,2,32]{0,2,1:T(8,128)(2,1)S(1)} %collective-permute-done.1) | copy-start | bytes 786436
  67.5 12.3 %collective-permute-start.2 = (bf16[2048,2,32]{0,2,1:T(8,128)(2,1)S(1)}, bf16[2048,2,32]{0,2,1:T(8,128)(2,1)S(1)}, u32[]{:S(2)}, u32[]{:S(2)}) collective-permute-start(bf16[2048,2,32]{0,2,1:T(8,128)(2,1)S(1)} %collective-permute-done.1), channel_id=1, source_target_pairs={{0,1},{1,2},{2,3},{3,4},{4,5},{5,6},{6,7},{7,8},{8,9},{9,10},{10,1... | collective-permute-start | bytes 786440 | tf_op jit(solution)/shard_map/ppermute | solution.py:93
  79.8 191.0 %copy-start.8 = (bf16[2048,2,32]{0,2,1:T(8,128)(2,1)}, bf16[2048,2,32]{0,2,1:T(8,128)(2,1)S(1)}, u32[]{:S(2)}) copy-start(bf16[2048,2,32]{0,2,1:T(8,128)(2,1)S(1)} %collective-permute-done.2) | copy-start | bytes 786436
  79.8 11.6 %collective-permute-start.3 = (bf16[2048,2,32]{0,2,1:T(8,128)(2,1)S(1)}, bf16[2048,2,32]{0,2,1:T(8,128)(2,1)S(1)}, u32[]{:S(2)}, u32[]{:S(2)}) collective-permute-start(bf16[2048,2,32]{0,2,1:T(8,128)(2,1)S(1)} %collective-permute-done.2), channel_id=1, source_target_pairs={{0,1},{1,2},{2,3},{3,4},{4,5},{5,6},{6,7},{7,8},{8,9},{9,10},{10,1... | collective-permute-start | bytes 786440 | tf_op jit(solution)/shard_map/ppermute | solution.py:93
  91.4 179.4 %copy-start.9 = (bf16[2048,2,32]{0,2,1:T(8,128)(2,1)}, bf16[2048,2,32]{0,2,1:T(8,128)(2,1)S(1)}, u32[]{:S(2)}) copy-start(bf16[2048,2,32]{0,2,1:T(8,128)(2,1)S(1)} %collective-permute-done.3) | copy-start | bytes 786436
  91.4 11.7 %collective-permute-start.4 = (bf16[2048,2,32]{0,2,1:T(8,128)(2,1)S(1)}, bf16[2048,2,32]{0,2,1:T(8,128)(2,1)S(1)}, u32[]{:S(2)}, u32[]{:S(2)}) collective-permute-start(bf16[2048,2,32]{0,2,1:T(8,128)(2,1)S(1)} %collective-permute-done.3), channel_id=1, source_target_pairs={{0,1},{1,2},{2,3},{3,4},{4,5},{5,6},{6,7},{7,8},{8,9},{9,10},{10,1... | collective-permute-start | bytes 786440 | tf_op jit(solution)/shard_map/ppermute | solution.py:93
  103.1 170.6 %copy-start.10 = (bf16[2048,2,32]{0,2,1:T(8,128)(2,1)}, bf16[2048,2,32]{0,2,1:T(8,128)(2,1)S(1)}, u32[]{:S(2)}) copy-start(bf16[2048,2,32]{0,2,1:T(8,128)(2,1)S(1)} %collective-permute-done.4) | copy-start | bytes 786436
  103.1 15.1 %collective-permute-start.5 = (bf16[2048,2,32]{0,2,1:T(8,128)(2,1)S(1)}, bf16[2048,2,32]{0,2,1:T(8,128)(2,1)S(1)}, u32[]{:S(2)}, u32[]{:S(2)}) collective-permute-start(bf16[2048,2,32]{0,2,1:T(8,128)(2,1)S(1)} %collective-permute-done.4), channel_id=1, source_target_pairs={{0,1},{1,2},{2,3},{3,4},{4,5},{5,6},{6,7},{7,8},{8,9},{9,10},{10,1... | collective-permute-start | bytes 786440 | tf_op jit(solution)/shard_map/ppermute | solution.py:93
  118.9 11.6 %collective-permute-start.6 = (bf16[2048,2,32]{0,2,1:T(8,128)(2,1)S(1)}, bf16[2048,2,32]{0,2,1:T(8,128)(2,1)S(1)}, u32[]{:S(2)}, u32[]{:S(2)}) collective-permute-start(bf16[2048,2,32]{0,2,1:T(8,128)(2,1)S(1)} %collective-permute-done.5), channel_id=1, source_target_pairs={{0,1},{1,2},{2,3},{3,4},{4,5},{5,6},{6,7},{7,8},{8,9},{9,10},{10,1... | collective-permute-start | bytes 786440 | tf_op jit(solution)/shard_map/ppermute | solution.py:93
  131.2 17.8 %collective-permute-start.7 = (bf16[2048,2,32]{0,2,1:T(8,128)(2,1)S(1)}, bf16[2048,2,32]{0,2,1:T(8,128)(2,1)S(1)}, u32[]{:S(2)}, u32[]{:S(2)}) collective-permute-start(bf16[2048,2,32]{0,2,1:T(8,128)(2,1)S(1)} %collective-permute-done.6), channel_id=1, source_target_pairs={{0,1},{1,2},{2,3},{3,4},{4,5},{5,6},{6,7},{7,8},{8,9},{9,10},{10,1... | collective-permute-start | bytes 786440 | tf_op jit(solution)/shard_map/ppermute | solution.py:93
  149.6 17.5 %collective-permute-start.8 = (bf16[2048,2,32]{0,2,1:T(8,128)(2,1)S(1)}, bf16[2048,2,32]{0,2,1:T(8,128)(2,1)S(1)}, u32[]{:S(2)}, u32[]{:S(2)}) collective-permute-start(bf16[2048,2,32]{0,2,1:T(8,128)(2,1)S(1)} %collective-permute-done.7), channel_id=1, source_target_pairs={{0,1},{1,2},{2,3},{3,4},{4,5},{5,6},{6,7},{7,8},{8,9},{9,10},{10,1... | collective-permute-start | bytes 786440 | tf_op jit(solution)/shard_map/ppermute | solution.py:93
  167.8 17.2 %collective-permute-start.9 = (bf16[2048,2,32]{0,2,1:T(8,128)(2,1)S(1)}, bf16[2048,2,32]{0,2,1:T(8,128)(2,1)S(1)}, u32[]{:S(2)}, u32[]{:S(2)}) collective-permute-start(bf16[2048,2,32]{0,2,1:T(8,128)(2,1)S(1)} %collective-permute-done.8), channel_id=1, source_target_pairs={{0,1},{1,2},{2,3},{3,4},{4,5},{5,6},{6,7},{7,8},{8,9},{9,10},{10,1... | collective-permute-start | bytes 786440 | tf_op jit(solution)/shard_map/ppermute | solution.py:93
  185.8 11.6 %collective-permute-start.10 = (bf16[2048,2,32]{0,2,1:T(8,128)(2,1)S(1)}, bf16[2048,2,32]{0,2,1:T(8,128)(2,1)S(1)}, u32[]{:S(2)}, u32[]{:S(2)}) collective-permute-start(bf16[2048,2,32]{0,2,1:T(8,128)(2,1)S(1)} %collective-permute-done.9), channel_id=1, source_target_pairs={{0,1},{1,2},{2,3},{3,4},{4,5},{5,6},{6,7},{7,8},{8,9},{9,10},{10,1... | collective-permute-start | bytes 786440 | tf_op jit(solution)/shard_map/ppermute | solution.py:93
  198.0 12.7 %collective-permute-start.11 = (bf16[2048,2,32]{0,2,1:T(8,128)(2,1)S(1)}, bf16[2048,2,32]{0,2,1:T(8,128)(2,1)S(1)}, u32[]{:S(2)}, u32[]{:S(2)}) collective-permute-start(bf16[2048,2,32]{0,2,1:T(8,128)(2,1)S(1)} %collective-permute-done.10), channel_id=1, source_target_pairs={{0,1},{1,2},{2,3},{3,4},{4,5},{5,6},{6,7},{7,8},{8,9},{9,10},{10,1... | collective-permute-start | bytes 786440 | tf_op jit(solution)/shard_map/ppermute | solution.py:93
  211.4 13.9 %collective-permute-start.12 = (bf16[2048,2,32]{0,2,1:T(8,128)(2,1)S(1)}, bf16[2048,2,32]{0,2,1:T(8,128)(2,1)S(1)}, u32[]{:S(2)}, u32[]{:S(2)}) collective-permute-start(bf16[2048,2,32]{0,2,1:T(8,128)(2,1)S(1)} %collective-permute-done.11), channel_id=1, source_target_pairs={{0,1},{1,2},{2,3},{3,4},{4,5},{5,6},{6,7},{7,8},{8,9},{9,10},{10,1... | collective-permute-start | bytes 786440 | tf_op jit(solution)/shard_map/ppermute | solution.py:93
  226.0 13.5 %collective-permute-start.13 = (bf16[2048,2,32]{0,2,1:T(8,128)(2,1)S(1)}, bf16[2048,2,32]{0,2,1:T(8,128)(2,1)}, u32[]{:S(2)}, u32[]{:S(2)}) collective-permute-start(bf16[2048,2,32]{0,2,1:T(8,128)(2,1)S(1)} %collective-permute-done.12), channel_id=1, source_target_pairs={{0,1},{1,2},{2,3},{3,4},{4,5},{5,6},{6,7},{7,8},{8,9},{9,10},{10,1... | collective-permute-start | bytes 786440 | tf_op jit(solution)/shard_map/ppermute | solution.py:93
  239.4 78.4 %collective-permute-start.14 = (bf16[2048,2,32]{0,2,1:T(8,128)(2,1)}, bf16[2048,2,32]{0,2,1:T(8,128)(2,1)}, u32[]{:S(2)}, u32[]{:S(2)}) collective-permute-start(bf16[2048,2,32]{0,2,1:T(8,128)(2,1)} %collective-permute-done.13), channel_id=1, source_target_pairs={{0,1},{1,2},{2,3},{3,4},{4,5},{5,6},{6,7},{7,8},{8,9},{9,10},{10,1... | collective-permute-start | bytes 786440 | tf_op jit(solution)/shard_map/ppermute | solution.py:93
  502.6 5.7 collective-permute-start.15
  506.0 5.8 collective-permute-start.16
  519.3 76.2 %copy-start.20 = (f32[4,16,128]{2,1,0:T(8,128)S(1)}, f32[4,16,128]{2,1,0:T(8,128)}, u32[]{:S(2)}) copy-start(f32[4,16,128]{2,1,0:T(8,128)} %get-tuple-element.185) | copy-start | bytes 98308
  519.3 76.9 %copy-start.3 = (bf16[2048,1,128]{0,2,1:T(8,128)(2,1)S(1)}, bf16[2048,1,128]{0,2,1:T(8,128)(2,1)}, u32[]{:S(2)}) copy-start(bf16[2048,1,128]{0,2,1:T(8,128)(2,1)} %get-tuple-element.184) | copy-start | bytes 1572868
  666.9 5.5 collective-permute-start.17
  672.5 7.0 collective-permute-start.18
  (22 other events, 142.5 us)
Sparse Core Ops, SparseCore 0:
  9.5 69.3 all-gather.6
  81.9 103.6 all-gather.8
  548.9 71.9 all-gather.10
